TPU v7x, 128 devices: a whole 4x4x4 slice. The times are simulated.
128 devices in a mesh: sub: 16 (over z, y), col: 8 (over x, core).
Axes of the slice: x: 4, y: 4, z: 4, core: 2. Of those that a mesh axis runs over, the one named last changes fastest.
Arguments:
- z_basis: bfloat16 [32, 16, 6, 64, 4096], P('sub', 'col'), may hold values from -6 to 6
- jac_center: bfloat16 [32, 16, 6, 6, 4096], P('sub', 'col'), may hold values from -0.0234375 to 0.0234375
- jac_lower: bfloat16 [32, 16, 6, 6, 4096], P('sub', 'col'), may hold values from -0.0234375 to 0.0234375
- jac_upper: bfloat16 [32, 16, 6, 6, 4096], P('sub', 'col'), may hold values from -0.0234375 to 0.0234375
- face_cells: int32 [32, 16, 4, 128], P('sub', 'col'), may hold values from 0 to 4095
- couple: bfloat16 [32, 16, 4, 6, 6, 128], P('sub', 'col'), may hold values from -0.21875 to 0.21875
Outputs:
- diag_tiles: float32 [32, 16, 64, 64], P('sub', 'col')
- off_tiles: float32 [32, 16, 4, 64, 64], P('sub', 'col')
All inputs are finite; a program needn't handle non-finite values.
Results may differ from a plain program's by a relative error of at most 0.0029.
Values may be sent and summed in bfloat16 or wider, within the bound.
A program may use at most 192 MiB of HBM per device.

v0:
```python
import functools

import jax
import jax.numpy as jnp
from jax import lax
from jax.experimental import pallas as pl
from jax.experimental.pallas import tpu as pltpu
from jax.sharding import PartitionSpec as P

MESH = pl.DeviceIdType.MESH
F32 = jnp.float32
BF16 = jnp.bfloat16
NT = (((1,), (1,)), ((), ()))
ROWS = 8
LANES = 128
WIDE = 256
PIECE = 512
OPPOSITE = (1, 0, 3, 2)


def neighbour_of(facing):
    sub, col = lax.axis_index("sub"), lax.axis_index("col")
    subs, cols = lax.axis_size("sub"), lax.axis_size("col")
    if facing == 0:
        return lax.rem(sub + 1, subs), col
    if facing == 1:
        return lax.rem(sub + subs - 1, subs), col
    if facing == 2:
        return sub, lax.rem(col + 1, cols)
    return sub, lax.rem(col + cols - 1, cols)


def has_neighbour(facing):
    sub, col = lax.axis_index("sub"), lax.axis_index("col")
    if facing == 0:
        return sub < lax.axis_size("sub") - 1
    if facing == 1:
        return sub > 0
    if facing == 2:
        return col < lax.axis_size("col") - 1
    return col > 0


def kernel(dims, z_hbm, jc_hbm, jl_hbm, ju_hbm, cells_ref, couple_ref, diag_ref, off_ref,
           z, jac, coef, applied, gather, faces, pushed, arrived, load_sem, send_sem, recv_sem):
    nx, ny, comp, kdim, ncell, nface = dims
    subs = nx * ny
    chunks = ncell // WIDE
    tiles = [(t, k0) for t in range(WIDE // LANES) for k0 in range(0, kdim, ROWS)]

    def loads(s):
        pairs = [(z_hbm.at[s], z.at[s])]
        pairs += [(ref.at[s], jac.at[s, n]) for n, ref in enumerate((jc_hbm, jl_hbm, ju_hbm))]
        return [pltpu.make_async_copy(src, dst, load_sem.at[s, n]) for n, (src, dst) in enumerate(pairs)]

    for s in range(subs):
        for copy in loads(s):
            copy.start()
    barrier = pltpu.get_barrier_semaphore()
    for facing in range(4):
        pl.semaphore_signal(barrier, inc=1, device_id=neighbour_of(facing), device_id_type=MESH)

    diag_ref[...] = jnp.zeros_like(diag_ref)
    applied[1] = jnp.zeros_like(applied[1])

    lane = lax.broadcasted_iota(jnp.int32, (ROWS, LANES), 1)
    first, last = lane == 0, lane == LANES - 1

    def chunk(n, side, extra):
        s = n // chunks
        c0 = pl.multiple_of(lax.rem(n, chunks) * WIDE, WIDE)
        cell = lax.broadcasted_iota(jnp.int32, (comp, WIDE), 1) + c0
        for a in range(comp):
            for d in range(3):
                block = jac[s, d, a, :, pl.ds(c0, WIDE)].astype(F32)
                if d == 1:
                    block = jnp.where(cell == 0, 0.0, block)
                if d == 2:
                    block = jnp.where(cell == ncell - 1, 0.0, block)
                coef[side, d * comp + a, 0:comp] = block
        past = jnp.maximum(n - 1, 0)
        sp = past // chunks
        cq = pl.multiple_of(lax.rem(past, chunks) * WIDE, WIDE)
        total = []

        def tile_dot(a):
            total.append(
                lax.dot_general(
                    applied[1 - side, a], z[sp, a, :, pl.ds(cq, WIDE)], NT, preferred_element_type=F32
                )
            )

        slots = {}
        for a in range(comp):
            slots.setdefault(a * len(tiles) // comp, []).append(functools.partial(tile_dot, a))
        for m, step in enumerate(extra):
            slots.setdefault((2 * m + 1) * len(tiles) // (2 * len(extra)), []).append(step)

        for m, (t, k0) in enumerate(tiles):
            for step in slots.get(m, []):
                step()
            cc = pl.multiple_of(c0 + t * LANES, LANES)
            cm = pl.multiple_of(jnp.maximum(cc - LANES, 0), LANES)
            cp = pl.multiple_of(jnp.minimum(cc + LANES, ncell - LANES), LANES)
            values = []
            for b in range(comp):
                here = z[s, b, k0 : k0 + ROWS, pl.ds(cc, LANES)]
                low = jnp.where(last, z[s, b, k0 : k0 + ROWS, pl.ds(cm, LANES)], here)
                high = jnp.where(first, z[s, b, k0 : k0 + ROWS, pl.ds(cp, LANES)], here)
                values.append(
                    (
                        here.astype(F32),
                        pltpu.roll(low.astype(F32), 1, 1),
                        pltpu.roll(high.astype(F32), LANES - 1, 1),
                    )
                )
            for a in range(comp):
                acc = None
                for b in range(comp):
                    for d in range(3):
                        weight = coef[side, d * comp + a, b : b + 1, t * LANES : (t + 1) * LANES]
                        term = weight * values[b][d]
                        acc = term if acc is None else acc + term
                applied[side, a, k0 : k0 + ROWS, t * LANES : (t + 1) * LANES] = acc.astype(BF16)
        diag_ref[sp] += functools.reduce(lambda p, q: p + q, total)

    def with_faces(it, carry):
        for s in range(1, subs):
            @pl.when(it == s * 4)
            def _():
                for copy in loads(s):
                    copy.wait()

        fs = it // 4
        pair = lax.rem(it, 4) // 2
        half = lax.rem(it, 2)
        wanted = jnp.concatenate(
            [cells_ref[fs, pl.ds(2 * pair, 1)], cells_ref[fs, pl.ds(2 * pair + 1, 1)]], axis=1
        )

        def piece(h):
            k0 = pl.multiple_of(half * (ncell // 2) + h * PIECE, PIECE)
            position = lax.broadcasted_iota(jnp.int32, (PIECE, 2 * nface), 0)
            pick = jnp.where(position == wanted - k0, 1.0, 0.0).astype(BF16)
            part = jnp.dot(
                z[fs, :, :, pl.ds(k0, PIECE)].reshape(comp * kdim, PIECE), pick, preferred_element_type=F32
            )
            if h == 0:
                part = part + jnp.where(half == 0, 0.0, gather[...])
            else:
                part = part + gather[...]
            gather[...] = part
            if h == ncell // 2 // PIECE - 1:
                for b in range(comp):
                    for e in range(2):
                        faces[fs, 2 * pair + e, :, b * nface : (b + 1) * nface] = part[
                            b * kdim : (b + 1) * kdim, e * nface : (e + 1) * nface
                        ].astype(BF16)

        steps = [functools.partial(piece, h) for h in range(ncell // 2 // PIECE)]
        chunk(2 * it, 0, steps[: len(steps) // 2])
        chunk(2 * it + 1, 1, steps[len(steps) // 2 :])
        return carry

    def without_faces(it, carry):
        chunk(2 * it, 0, [])
        chunk(2 * it + 1, 1, [])
        return carry

    for copy in loads(0):
        copy.wait()
    half_way = subs * chunks // 4
    lax.fori_loop(0, half_way, with_faces, 0)

    def push(q, carry):
        s, d = q // 4, lax.rem(q, 4)
        picked = [faces[s, d, :, b * nface : (b + 1) * nface].astype(F32) for b in range(comp)]
        for a in range(comp):
            weights = couple_ref[s, d, a].astype(F32)
            acc = None
            for b in range(comp):
                term = weights[b : b + 1] * picked[b]
                acc = term if acc is None else acc + term
            pushed[s, d, :, a * nface : (a + 1) * nface] = acc.astype(BF16)
        return carry

    lax.fori_loop(0, subs * 4, push, 0)

    pl.semaphore_wait(barrier, 4)

    def sources(d):
        if d == 0:
            return [(nx - 1) * ny + j for j in range(ny)]
        if d == 1:
            return list(range(ny))
        if d == 2:
            return [i * ny + ny - 1 for i in range(nx)]
        return [i * ny for i in range(nx)]

    sends = []
    for d in range(4):
        for m, s in enumerate(sources(d)):
            sends.append(
                pltpu.make_async_remote_copy(
                    src_ref=pushed.at[s, d],
                    dst_ref=arrived.at[d, m],
                    send_sem=send_sem.at[d, m],
                    recv_sem=recv_sem.at[d, m],
                    device_id=neighbour_of(d),
                    device_id_type=MESH,
                )
            )
    for copy in sends:
        copy.start()

    lax.fori_loop(half_way, 2 * half_way, without_faces, 0)

    final = functools.reduce(
        lambda p, q: p + q,
        [
            lax.dot_general(applied[1, a], z[subs - 1, a, :, ncell - WIDE :], NT, preferred_element_type=F32)
            for a in range(comp)
        ],
    )
    diag_ref[subs - 1] += final
    for s in range(subs):
        diag_ref[s] = diag_ref[s].T

    def tile(s, e, right):
        return lax.dot_general(faces[s, e], right, NT, preferred_element_type=F32)

    steps_of = ((1, 0), (-1, 0), (0, 1), (0, -1))
    for i in range(nx):
        for j in range(ny):
            for e in range(4):
                ti, tj = i + steps_of[e][0], j + steps_of[e][1]
                if 0 <= ti < nx and 0 <= tj < ny:
                    off_ref[i * ny + j, e] = tile(i * ny + j, e, pushed[ti * ny + tj, OPPOSITE[e]])
    for copy in sends:
        copy.wait()
    for e in range(4):
        d = OPPOSITE[e]
        inside = has_neighbour(e)
        for m, s in enumerate(sources(e)):
            off_ref[s, e] = jnp.where(inside, tile(s, e, arrived[d, m]), 0.0)


def on_device(z_basis, jac_center, jac_lower, jac_upper, face_cells, couple):
    nx, ny, comp, kdim, ncell = z_basis.shape
    nface = face_cells.shape[-1]
    subs = nx * ny
    rank = lambda array: array.reshape((subs,) + array.shape[2:])
    wide = comp * nface
    diag, off = pl.pallas_call(
        functools.partial(kernel, (nx, ny, comp, kdim, ncell, nface)),
        out_shape=(
            jax.ShapeDtypeStruct((subs, kdim, kdim), F32),
            jax.ShapeDtypeStruct((subs, 4, kdim, kdim), F32),
        ),
        in_specs=[pl.BlockSpec(memory_space=pl.ANY)] * 4 + [pl.BlockSpec(memory_space=pltpu.VMEM)] * 2,
        out_specs=[pl.BlockSpec(memory_space=pltpu.VMEM)] * 2,
        scratch_shapes=[
            pltpu.VMEM((subs, comp, kdim, ncell), BF16),
            pltpu.VMEM((subs, 3, comp, comp, ncell), BF16),
            pltpu.VMEM((2, 3 * comp, 8, WIDE), F32),
            pltpu.VMEM((2, comp, kdim, WIDE), BF16),
            pltpu.VMEM((comp * kdim, 2 * nface), F32),
            pltpu.VMEM((subs, 4, kdim, wide), BF16),
            pltpu.VMEM((subs, 4, kdim, wide), BF16),
            pltpu.VMEM((4, 2, kdim, wide), BF16),
            pltpu.SemaphoreType.DMA((subs, 4)),
            pltpu.SemaphoreType.DMA((4, 2)),
            pltpu.SemaphoreType.DMA((4, 2)),
        ],
        compiler_params=pltpu.CompilerParams(
            collective_id=0, has_side_effects=True, vmem_limit_bytes=56 * 2**20
        ),
        cost_estimate=pl.CostEstimate(flops=10**10, bytes_accessed=17 * 10**6, transcendentals=0),
    )(*(rank(x) for x in (z_basis, jac_center, jac_lower, jac_upper, face_cells, couple)))
    return diag.reshape(nx, ny, kdim, kdim), off.reshape(nx, ny, 4, kdim, kdim)


def solution(mesh):
    in_specs = (
        P("sub", "col", None, None, None),
        P("sub", "col", None, None, None),
        P("sub", "col", None, None, None),
        P("sub", "col", None, None, None),
        P("sub", "col", None, None),
        P("sub", "col", None, None, None, None),
    )
    out_specs = (P("sub", "col", None, None), P("sub", "col", None, None, None))
    return jax.shard_map(
        on_device, mesh=mesh, in_specs=in_specs, out_specs=out_specs, check_vma=False
    )
```

profile of v0, /device:TPU:3, one launch (start us, length us, event | category | flops | bytes accessed | tf_op | source)
XLA Modules:
  0.0 71.3 jit_solution(958844597285546701)
XLA Ops:
  0.6 0.0 copy-start
  0.6 1.7 %copy.11 = bf16[2,2,4,6,6,128]{5,4,3,2,1,0:T(8,128)(2,1)} copy(bf16[2,2,4,6,6,128]{5,2,4,3,1,0:T(4,128)(2,1)} %param.11) | data formatting | bytes 294912 | tf_op args[5]
  2.4 3.1 %copy.8 = bf16[2,2,6,6,4096]{4,3,2,1,0:T(8,128)(2,1)} copy(bf16[2,2,6,6,4096]{4,1,3,2,0:T(2,128)(2,1)} %param.7) | data formatting | bytes 2359296 | tf_op args[1]
  5.5 0.0 copy-start.1
  5.5 0.0 copy-done
  5.5 1.8 %copy.9 = bf16[2,2,6,6,4096]{4,3,2,1,0:T(8,128)(2,1)} copy(bf16[2,2,6,6,4096]{4,1,3,2,0:T(2,128)(2,1)S(1)} %copy-done) | data formatting | bytes 2359296 | tf_op args[2]
  7.3 0.0 copy-done.1
  7.3 1.8 %copy.10 = bf16[2,2,6,6,4096]{4,3,2,1,0:T(8,128)(2,1)} copy(bf16[2,2,6,6,4096]{4,1,3,2,0:T(2,128)(2,1)S(1)} %copy-done.1) | data formatting | bytes 2359296 | tf_op args[3]
  9.2 58.7 %shard_map.77 = (f32[4,64,64]{2,1,0:T(8,128)}, f32[4,4,64,64]{3,2,1,0:T(8,128)}) custom-call(bf16[4,6,64,4096]{3,2,1,0:T(8,128)(2,1)} %bitcast.14, bf16[4,6,6,4096]{3,2,1,0:T(8,128)(2,1)} %bitcast.8, bf16[4,6,6,4096]{3,2,1,0:T(8,128)(2,1)} %bitcast.9, bf16[4,6,6,4096]{3,2,1,0:T(8,128)(2,1)} %bitcast.10, s32[4,4,128]{2,1,0:T(4,128)} %bitcast.15, ...), custom_call_target="tpu_custom_call" | custom-call | flops 10000000000 | bytes 17000000 | tf_op jit(solution)/shard_map/pallas_call | solution.py:254
  67.9 1.6 %copy.14 = f32[2,2,64,64]{3,2,1,0:T(8,128)} copy(f32[2,2,64,64]{3,2,1,0:T(8,128)} %bitcast.13) | data formatting | bytes 131072
  69.5 1.9 %copy.15 = f32[2,2,4,64,64]{4,3,2,1,0:T(8,128)} copy(f32[2,2,4,64,64]{4,3,2,1,0:T(8,128)} %bitcast.11) | data formatting | bytes 524288
Async XLA Ops:
  0.6 4.9 %copy-start = (bf16[2,2,6,6,4096]{4,1,3,2,0:T(2,128)(2,1)S(1)}, bf16[2,2,6,6,4096]{4,1,3,2,0:T(2,128)(2,1)}, u32[]{:S(2)}) copy-start(bf16[2,2,6,6,4096]{4,1,3,2,0:T(2,128)(2,1)} %param.8) | copy-start | bytes 3538948
  5.5 1.8 %copy-start.1 = (bf16[2,2,6,6,4096]{4,1,3,2,0:T(2,128)(2,1)S(1)}, bf16[2,2,6,6,4096]{4,1,3,2,0:T(2,128)(2,1)}, u32[]{:S(2)}) copy-start(bf16[2,2,6,6,4096]{4,1,3,2,0:T(2,128)(2,1)} %param.9) | copy-start | bytes 3538948
where the time goes:
time: 71.6 us; the launch traced here: 71.3 us
  Pallas kernels  58.7 us (82%)
  local copies, waits for them, and re-layouts  12 us (17%)
    pallas_call x1, Pallas kernels, on_device(): pl.pallas_call(functools.partial(kernel, (nx, ny, comp, kdim, ncell, nfac...  58.7 us
    unnamed x10, local copies, waits for them, and re-layouts  12 us

commit v1 on v0

v1 whole, which is shorter than its diff:
```python
import functools

import jax
import jax.numpy as jnp
from jax import lax
from jax.experimental import pallas as pl
from jax.experimental.pallas import tpu as pltpu
from jax.sharding import PartitionSpec as P

MESH = pl.DeviceIdType.MESH
F32 = jnp.float32
BF16 = jnp.bfloat16
NT = (((1,), (1,)), ((), ()))
ROWS = 8
LANES = 128
WIDE = 256
PIECE = 512
OPPOSITE = (1, 0, 3, 2)


def neighbour_of(facing):
    sub, col = lax.axis_index("sub"), lax.axis_index("col")
    subs, cols = lax.axis_size("sub"), lax.axis_size("col")
    if facing == 0:
        return lax.rem(sub + 1, subs), col
    if facing == 1:
        return lax.rem(sub + subs - 1, subs), col
    if facing == 2:
        return sub, lax.rem(col + 1, cols)
    return sub, lax.rem(col + cols - 1, cols)


def has_neighbour(facing):
    sub, col = lax.axis_index("sub"), lax.axis_index("col")
    if facing == 0:
        return sub < lax.axis_size("sub") - 1
    if facing == 1:
        return sub > 0
    if facing == 2:
        return col < lax.axis_size("col") - 1
    return col > 0


def kernel(dims, z_hbm, jc_hbm, jl_hbm, ju_hbm, cells_ref, couple_ref, diag_ref, off_ref,
           z, jac, coef, applied, gather, faces, pushed, arrived, load_sem, send_sem, recv_sem):
    nx, ny, comp, kdim, ncell, nface = dims
    subs = nx * ny
    chunks = ncell // WIDE
    quarter = ncell // 4
    tiles = [(t, k0) for t in range(WIDE // LANES) for k0 in range(0, kdim, ROWS)]

    def loads(n):
        i, at = n // 4, pl.multiple_of(lax.rem(n, 4) * quarter, quarter)
        pairs = [
            (z_hbm.at[i * ny + j, :, :, pl.ds(at, quarter)], z.at[i * ny + j, :, :, pl.ds(LANES + at, quarter)])
            for j in range(ny)
        ]
        pairs += [
            (ref.at[i, :, :, :, pl.ds(at, quarter)], jac.at[m, i, :, :, :, pl.ds(at, quarter)])
            for m, ref in enumerate((jc_hbm, jl_hbm, ju_hbm))
        ]
        return [pltpu.make_async_copy(src, dst, load_sem.at[n, m]) for m, (src, dst) in enumerate(pairs)]

    for n in range(4 * nx):
        for copy in loads(n):
            copy.start()
    barrier = pltpu.get_barrier_semaphore()
    for facing in range(4):
        pl.semaphore_signal(barrier, inc=1, device_id=neighbour_of(facing), device_id_type=MESH)

    diag_ref[...] = jnp.zeros_like(diag_ref)
    applied[1] = jnp.zeros_like(applied[1])
    zero = jnp.zeros((comp, kdim, LANES), BF16)
    for s in range(subs):
        z[s, :, :, 0:LANES] = zero
        z[s, :, :, LANES + ncell :] = zero

    lane = lax.broadcasted_iota(jnp.int32, (ROWS, LANES), 1)
    first, last = lane == 0, lane == LANES - 1

    def stencil(it, side, extra):
        i = it // chunks
        s = i * ny + side
        c0 = pl.multiple_of(lax.rem(it, chunks) * WIDE, WIDE)
        past = it if side else jnp.maximum(it - 1, 0)
        sp = past // chunks * ny + 1 - side
        cq = pl.multiple_of(lax.rem(past, chunks) * WIDE + LANES, LANES)
        total = []

        def tile_dot(a):
            total.append(
                lax.dot_general(
                    applied[1 - side, a], z[sp, a, :, pl.ds(cq, WIDE)], NT, preferred_element_type=F32
                )
            )

        slots = {}
        for a in range(comp):
            slots.setdefault(a * len(tiles) // comp, []).append(functools.partial(tile_dot, a))
        for m, step in enumerate(extra):
            slots.setdefault((2 * m + 1) * len(tiles) // (2 * len(extra)), []).append(step)

        for m, (t, k0) in enumerate(tiles):
            for step in slots.get(m, []):
                step()
            at = pl.multiple_of(c0 + (t + 1) * LANES, LANES)
            values = []
            for b in range(comp):
                here = z[s, b, k0 : k0 + ROWS, pl.ds(at, LANES)]
                low = jnp.where(last, z[s, b, k0 : k0 + ROWS, pl.ds(at - LANES, LANES)], here)
                high = jnp.where(first, z[s, b, k0 : k0 + ROWS, pl.ds(at + LANES, LANES)], here)
                values.append(
                    (
                        here.astype(F32),
                        pltpu.roll(low.astype(F32), 1, 1),
                        pltpu.roll(high.astype(F32), LANES - 1, 1),
                    )
                )
            for a in range(comp):
                acc = None
                for b in range(comp):
                    for d in range(3):
                        weight = coef[d, a, b, side : side + 1, t * LANES : (t + 1) * LANES]
                        term = weight * values[b][d]
                        acc = term if acc is None else acc + term
                applied[side, a, k0 : k0 + ROWS, t * LANES : (t + 1) * LANES] = acc.astype(BF16)
        diag_ref[sp] += functools.reduce(lambda p, q: p + q, total)

    def weights(it):
        i = it // chunks
        c0 = pl.multiple_of(lax.rem(it, chunks) * WIDE, WIDE)
        for d in range(3):
            for a in range(comp):
                coef[d, a] = jac[d, i, a, :, :, pl.ds(c0, WIDE)].astype(F32)

    def with_faces(it, carry):
        @pl.when((lax.rem(it, 2) == 1) & (it < 8 * nx - 1))
        def _():
            for copy in loads((it + 1) // 2):
                copy.wait()

        i = it // 8
        fs = i * ny + lax.rem(it, 2)
        block = lax.rem(it, 8) // 2

        def piece(h):
            pair, k = h % 2, h // 2
            k0 = pl.multiple_of(block * quarter + k * PIECE, PIECE)
            wanted = jnp.concatenate(
                [cells_ref[fs, 2 * pair : 2 * pair + 1], cells_ref[fs, 2 * pair + 1 : 2 * pair + 2]], axis=1
            )
            position = lax.broadcasted_iota(jnp.int32, (PIECE, 2 * nface), 0)
            pick = jnp.where(position == wanted - k0, 1.0, 0.0).astype(BF16)
            part = jnp.dot(
                z[fs, :, :, pl.ds(pl.multiple_of(k0 + LANES, LANES), PIECE)].reshape(comp * kdim, PIECE),
                pick,
                preferred_element_type=F32,
            )
            if k == 0:
                gather[fs, pair] = part + jnp.where(block == 0, 0.0, gather[fs, pair])
            else:
                gather[fs, pair] += part

        steps = [functools.partial(piece, h) for h in range(2 * quarter // PIECE)]
        weights(it)
        stencil(it, 0, steps[: len(steps) // 2])
        stencil(it, 1, steps[len(steps) // 2 :])
        return carry

    def without_faces(it, carry):
        weights(it)
        stencil(it, 0, [])
        stencil(it, 1, [])
        return carry

    for copy in loads(0):
        copy.wait()
    lax.fori_loop(0, 8 * nx, with_faces, 0)

    def push(s, carry):
        for d in range(4):
            picked = []
            for b in range(comp):
                values = gather[s, d // 2, b * kdim : (b + 1) * kdim, (d % 2) * nface : (d % 2 + 1) * nface]
                faces[s, d, :, b * nface : (b + 1) * nface] = values.astype(BF16)
                picked.append(values)
            for a in range(comp):
                acc = None
                for b in range(comp):
                    term = couple_ref[s, a, b].astype(F32)[d : d + 1] * picked[b]
                    acc = term if acc is None else acc + term
                pushed[s, d, :, a * nface : (a + 1) * nface] = acc.astype(BF16)
        return carry

    lax.fori_loop(0, subs, push, 0)

    pl.semaphore_wait(barrier, 4)

    def sources(d):
        if d == 0:
            return [(nx - 1) * ny + j for j in range(ny)]
        if d == 1:
            return list(range(ny))
        if d == 2:
            return [i * ny + ny - 1 for i in range(nx)]
        return [i * ny for i in range(nx)]

    sends = []
    for d in range(4):
        for m, s in enumerate(sources(d)):
            sends.append(
                pltpu.make_async_remote_copy(
                    src_ref=pushed.at[s, d],
                    dst_ref=arrived.at[d, m],
                    send_sem=send_sem.at[d, m],
                    recv_sem=recv_sem.at[d, m],
                    device_id=neighbour_of(d),
                    device_id_type=MESH,
                )
            )
    for copy in sends:
        copy.start()

    lax.fori_loop(8 * nx, nx * chunks, without_faces, 0)

    final = functools.reduce(
        lambda p, q: p + q,
        [
            lax.dot_general(
                applied[1, a], z[subs - 1, a, :, LANES + ncell - WIDE : LANES + ncell], NT,
                preferred_element_type=F32,
            )
            for a in range(comp)
        ],
    )
    diag_ref[subs - 1] += final
    for s in range(subs):
        diag_ref[s] = diag_ref[s].T

    def tile(s, e, right):
        return lax.dot_general(faces[s, e], right, NT, preferred_element_type=F32)

    steps_of = ((1, 0), (-1, 0), (0, 1), (0, -1))
    for i in range(nx):
        for j in range(ny):
            for e in range(4):
                ti, tj = i + steps_of[e][0], j + steps_of[e][1]
                if 0 <= ti < nx and 0 <= tj < ny:
                    off_ref[i * ny + j, e] = tile(i * ny + j, e, pushed[ti * ny + tj, OPPOSITE[e]])
    for copy in sends:
        copy.wait()
    for e in range(4):
        d = OPPOSITE[e]
        inside = has_neighbour(e)
        for m, s in enumerate(sources(e)):
            off_ref[s, e] = jnp.where(inside, tile(s, e, arrived[d, m]), 0.0)


def hand_over(diag_in, off_in, diag_out, off_out, sem):
    copies = [
        pltpu.make_async_copy(src, dst, sem.at[n])
        for n, (src, dst) in enumerate(((diag_in, diag_out), (off_in, off_out)))
    ]
    for copy in copies:
        copy.start()
    for copy in copies:
        copy.wait()


def on_device(z_basis, jac_center, jac_lower, jac_upper, face_cells, couple):
    nx, ny, comp, kdim, ncell = z_basis.shape
    nface = face_cells.shape[-1]
    subs = nx * ny
    merge = lambda array: array.reshape((subs,) + array.shape[2:])
    paired = [jnp.transpose(array, (0, 2, 3, 1, 4)) for array in (jac_center, jac_lower, jac_upper)]
    wide = comp * nface
    shapes = (
        jax.ShapeDtypeStruct((subs, kdim, kdim), F32),
        jax.ShapeDtypeStruct((subs, 4, kdim, kdim), F32),
    )
    results = pl.pallas_call(
        functools.partial(kernel, (nx, ny, comp, kdim, ncell, nface)),
        out_shape=shapes,
        in_specs=[pl.BlockSpec(memory_space=pl.ANY)] * 4 + [pl.BlockSpec(memory_space=pltpu.VMEM)] * 2,
        out_specs=[pl.BlockSpec(memory_space=pltpu.VMEM)] * 2,
        scratch_shapes=[
            pltpu.VMEM((subs, comp, kdim, ncell + 2 * LANES), BF16),
            pltpu.VMEM((3, nx, comp, comp, ny, ncell), BF16),
            pltpu.VMEM((3, comp, comp, ny, WIDE), F32),
            pltpu.VMEM((2, comp, kdim, WIDE), BF16),
            pltpu.VMEM((subs, 2, comp * kdim, 2 * nface), F32),
            pltpu.VMEM((subs, 4, kdim, wide), BF16),
            pltpu.VMEM((subs, 4, kdim, wide), BF16),
            pltpu.VMEM((4, 2, kdim, wide), BF16),
            pltpu.SemaphoreType.DMA((4 * nx, 3 + ny)),
            pltpu.SemaphoreType.DMA((4, 2)),
            pltpu.SemaphoreType.DMA((4, 2)),
        ],
        compiler_params=pltpu.CompilerParams(
            collective_id=0, has_side_effects=True, vmem_limit_bytes=56 * 2**20
        ),
        cost_estimate=pl.CostEstimate(flops=10**10, bytes_accessed=17 * 10**6, transcendentals=0),
    )(
        merge(z_basis), *paired, merge(face_cells), merge(jnp.transpose(couple, (0, 1, 3, 4, 2, 5)))
    )
    diag, off = pl.pallas_call(
        hand_over,
        out_shape=shapes,
        in_specs=[pl.BlockSpec(memory_space=pl.ANY)] * 2,
        out_specs=[pl.BlockSpec(memory_space=pl.ANY)] * 2,
        scratch_shapes=[pltpu.SemaphoreType.DMA((2,))],
        compiler_params=pltpu.CompilerParams(vmem_limit_bytes=56 * 2**20),
    )(*results)
    return diag.reshape(nx, ny, kdim, kdim), off.reshape(nx, ny, 4, kdim, kdim)


def solution(mesh):
    in_specs = (
        P("sub", "col", None, None, None),
        P("sub", "col", None, None, None),
        P("sub", "col", None, None, None),
        P("sub", "col", None, None, None),
        P("sub", "col", None, None),
        P("sub", "col", None, None, None, None),
    )
    out_specs = (P("sub", "col", None, None), P("sub", "col", None, None, None))
    return jax.shard_map(
        on_device, mesh=mesh, in_specs=in_specs, out_specs=out_specs, check_vma=False
    )
```

time: 71.6 us -> 75.9 us (1.060)
  Pallas kernels: 58.7 us -> 75.2 us
  local copies, waits for them, and re-layouts: 12 us -> 0 us
    pallas_call x0 -> x1, Pallas kernels: none -> 21 us  [on_device(): pl.pallas_call(hand_over, out_shape=shapes, in_specs=[pl.BlockSpec(memory...]
    unnamed x10 -> x0, local copies, waits for them, and re-layouts: 12 us -> none
    pallas_call x1, Pallas kernels: 58.7 us -> 54.2 us  [on_device(): pl.pallas_call(functools.partial(kernel, (nx, ny, comp, kdim, ncell, nfac...]
where the time goes in v1:
time: 75.9 us; the launch traced here: 75.8 us
  Pallas kernels  75.2 us (99%)
    pallas_call x1, Pallas kernels, on_device(): pl.pallas_call(functools.partial(kernel, (nx, ny, comp, kdim, ncell, nfac...  54.2 us
    pallas_call x1, Pallas kernels, on_device(): pl.pallas_call(hand_over, out_shape=shapes, in_specs=[pl.BlockSpec(memory...  21 us

profile of v1, /device:TPU:3, one launch (start us, length us, event | category | flops | bytes accessed | tf_op | source)
XLA Modules:
  0.0 75.8 jit_solution(14490221234994512790)
XLA Ops:
  0.6 54.2 %shard_map.77 = (f32[4,64,64]{2,1,0:T(8,128)}, f32[4,4,64,64]{3,2,1,0:T(8,128)}) custom-call(bf16[4,6,64,4096]{3,2,1,0:T(8,128)(2,1)} %bitcast.10, bf16[2,6,6,2,4096]{4,3,2,1,0:T(2,128)(2,1)} %bitcast.11, bf16[2,6,6,2,4096]{4,3,2,1,0:T(2,128)(2,1)} %bitcast.12, bf16[2,6,6,2,4096]{4,3,2,1,0:T(2,128)(2,1)} %bitcast.13, s32[4,4,128]{2,1,0:T(4,128)} %bitcast.17, ...), custom_call_target="tpu_custom_call" | custom-call | flops 10000000000 | bytes 17000000 | tf_op jit(solution)/shard_map/pallas_call | solution.py:281
  54.8 21.0 %shard_map.78 = (f32[4,64,64]{2,1,0:T(8,128)}, f32[4,4,64,64]{3,2,1,0:T(8,128)}) custom-call(f32[4,64,64]{2,1,0:T(8,128)} %get-tuple-element.6.diag_in, f32[4,4,64,64]{3,2,1,0:T(8,128)} %get-tuple-element.7.off_in), custom_call_target="tpu_custom_call" | custom-call | tf_op jit(solution)/shard_map/pallas_call | solution.py:306

commit v2 on v1

--- a/solution.py
+++ b/solution.py
@@ -47,7 +47,7 @@
     subs = nx * ny
     chunks = ncell // WIDE
     quarter = ncell // 4
-    tiles = [(t, k0) for t in range(WIDE // LANES) for k0 in range(0, kdim, ROWS)]
+    all_tiles = [(t, k0) for t in range(WIDE // LANES) for k0 in range(0, kdim, ROWS)]
 
     def loads(n):
         i, at = n // 4, pl.multiple_of(lax.rem(n, 4) * quarter, quarter)
@@ -77,6 +77,68 @@
 
     lane = lax.broadcasted_iota(jnp.int32, (ROWS, LANES), 1)
     first, last = lane == 0, lane == LANES - 1
+    place = lax.broadcasted_iota(jnp.int32, (16, 2 * nface), 0).astype(jnp.int16)
+    one, nil = jnp.ones((16, 2 * nface), BF16), jnp.zeros((16, 2 * nface), BF16)
+
+    row16 = lax.broadcasted_iota(jnp.int32, (16, LANES), 0)
+    col16 = lax.broadcasted_iota(jnp.int32, (16, LANES), 1)
+    phase = [lax.rem(row16 - col16 + (p + 3 * LANES), 3) for p in range(3)]
+    centred, ahead = [x == 0 for x in phase], [x == 1 for x in phase]
+    band = [
+        jnp.where(jnp.abs(row16 + 16 * r - col16) <= 1, 1.0, 0.0).astype(BF16) for r in range(LANES // 16)
+    ]
+
+    def matrix_tile(s, side, t, at):
+        span = slice(t * LANES, (t + 1) * LANES)
+        sums = [None] * (comp // 2)
+
+        def add(q, part):
+            sums[q] = part if sums[q] is None else sums[q] + part
+
+        def row(d, a, b, rows):
+            return jnp.broadcast_to(coef[d, a, b, side : side + 1, span], (rows, LANES))
+
+        def inner(q, m):
+            blocks = []
+            for b in (2 * m, 2 * m + 1):
+                line = []
+                for a in (2 * q, 2 * q + 1):
+                    mid, low, high = (row(d, a, b, 16).astype(BF16) for d in range(3))
+                    mixed = [jnp.where(centred[p], mid, jnp.where(ahead[p], high, low)) for p in range(3)]
+                    line.append(jnp.concatenate([mixed[r % 3] * band[r] for r in range(LANES // 16)], axis=0))
+                blocks.append(jnp.concatenate(line, axis=1))
+            pair = jnp.concatenate([z[s, b, :, pl.ds(at, LANES)] for b in (2 * m, 2 * m + 1)], axis=1)
+            add(q, jnp.dot(pair, jnp.concatenate(blocks, axis=0), preferred_element_type=F32))
+
+        def outer(qs):
+            across = lax.broadcasted_iota(jnp.int32, (kdim, LANES), 1)
+            edges = None
+            for b in range(comp):
+                ends = jnp.where(
+                    across == LANES - 1, z[s, b, :, pl.ds(at - LANES, LANES)], z[s, b, :, pl.ds(at + LANES, LANES)]
+                )
+                ends = pltpu.roll(ends.astype(F32), 2 * b + 1, 1)
+                edges = ends if edges is None else jnp.where(across < 2 * b, edges, ends)
+            edges = edges.astype(BF16)
+            for q in qs:
+                line = []
+                for a in (2 * q, 2 * q + 1):
+                    grid = jnp.zeros((16, LANES), F32)
+                    for b in range(comp):
+                        grid = jnp.where((row16 == 2 * b) & (col16 == 0), row(1, a, b, 16), grid)
+                        grid = jnp.where((row16 == 2 * b + 1) & (col16 == LANES - 1), row(2, a, b, 16), grid)
+                    line.append(jnp.concatenate([grid, jnp.zeros((LANES - 16, LANES), F32)], axis=0).astype(BF16))
+                add(q, jnp.dot(edges, jnp.concatenate(line, axis=1), preferred_element_type=F32))
+
+        def finish(q):
+            for e in range(2):
+                applied[side, 2 * q + e, :, span] = sums[q][:, e * LANES : (e + 1) * LANES].astype(BF16)
+
+        steps = [functools.partial(outer, range(comp // 2))]
+        for q in range(comp // 2):
+            steps += [functools.partial(inner, q, m) for m in range(comp // 2)]
+            steps.append(functools.partial(finish, q))
+        return steps
 
     def stencil(it, side, extra):
         i = it // chunks
@@ -94,7 +156,13 @@
                 )
             )
 
+        tiles = all_tiles
         slots = {}
+        if side == 0:
+            tiles = all_tiles[: len(all_tiles) // 2]
+            matrix = matrix_tile(s, side, 1, pl.multiple_of(c0 + 2 * LANES, LANES))
+            for m, step in enumerate(matrix):
+                slots.setdefault(m * len(tiles) // len(matrix), []).append(step)
         for a in range(comp):
             slots.setdefault(a * len(tiles) // comp, []).append(functools.partial(tile_dot, a))
         for m, step in enumerate(extra):
@@ -149,8 +217,10 @@
             wanted = jnp.concatenate(
                 [cells_ref[fs, 2 * pair : 2 * pair + 1], cells_ref[fs, 2 * pair + 1 : 2 * pair + 2]], axis=1
             )
-            position = lax.broadcasted_iota(jnp.int32, (PIECE, 2 * nface), 0)
-            pick = jnp.where(position == wanted - k0, 1.0, 0.0).astype(BF16)
+            near = jnp.broadcast_to(wanted - k0, (16, 2 * nface)).astype(jnp.int16)
+            pick = jnp.concatenate(
+                [jnp.where(place == near - 16 * r, one, nil) for r in range(PIECE // 16)], axis=0
+            )
             part = jnp.dot(
                 z[fs, :, :, pl.ds(pl.multiple_of(k0 + LANES, LANES), PIECE)].reshape(comp * kdim, PIECE),
                 pick,
@@ -163,8 +233,8 @@
 
         steps = [functools.partial(piece, h) for h in range(2 * quarter // PIECE)]
         weights(it)
-        stencil(it, 0, steps[: len(steps) // 2])
-        stencil(it, 1, steps[len(steps) // 2 :])
+        stencil(it, 0, steps[: len(steps) // 4])
+        stencil(it, 1, steps[len(steps) // 4 :])
         return carry
 
     def without_faces(it, carry):
@@ -256,15 +326,9 @@
             off_ref[s, e] = jnp.where(inside, tile(s, e, arrived[d, m]), 0.0)
 
 
-def hand_over(diag_in, off_in, diag_out, off_out, sem):
-    copies = [
-        pltpu.make_async_copy(src, dst, sem.at[n])
-        for n, (src, dst) in enumerate(((diag_in, diag_out), (off_in, off_out)))
-    ]
-    for copy in copies:
-        copy.start()
-    for copy in copies:
-        copy.wait()
+def hand_over(diag_in, off_in, diag_out, off_out):
+    diag_out[...] = diag_in[...]
+    off_out[...] = off_in[...]
 
 
 def on_device(z_basis, jac_center, jac_lower, jac_upper, face_cells, couple):
@@ -306,10 +370,8 @@
     diag, off = pl.pallas_call(
         hand_over,
         out_shape=shapes,
-        in_specs=[pl.BlockSpec(memory_space=pl.ANY)] * 2,
-        out_specs=[pl.BlockSpec(memory_space=pl.ANY)] * 2,
-        scratch_shapes=[pltpu.SemaphoreType.DMA((2,))],
-        compiler_params=pltpu.CompilerParams(vmem_limit_bytes=56 * 2**20),
+        in_specs=[pl.BlockSpec(memory_space=pltpu.VMEM)] * 2,
+        out_specs=[pl.BlockSpec(memory_space=pltpu.VMEM)] * 2,
     )(*results)
     return diag.reshape(nx, ny, kdim, kdim), off.reshape(nx, ny, 4, kdim, kdim)
 

time: 75.9 us -> 54.3 us (0.72)
  Pallas kernels: 75.2 us -> 53.5 us
    pallas_call x1, Pallas kernels: 21 us -> 1.96 us  [on_device(): pl.pallas_call(hand_over, out_shape=shapes, in_specs=[pl.BlockSpec(memory...]
    pallas_call x1, Pallas kernels: 54.2 us -> 51.6 us  [on_device(): pl.pallas_call(functools.partial(kernel, (nx, ny, comp, kdim, ncell, nfac...]
where the time goes in v2:
time: 54.3 us; the launch traced here: 54.2 us
  Pallas kernels  53.5 us (99%)
  between operations  0.64 us (1%)
    pallas_call x1, Pallas kernels, on_device(): pl.pallas_call(functools.partial(kernel, (nx, ny, comp, kdim, ncell, nfac...  51.6 us
    pallas_call x1, Pallas kernels, on_device(): pl.pallas_call(hand_over, out_shape=shapes, in_specs=[pl.BlockSpec(memory...  1.96 us

profile of v2, /device:TPU:3, one launch (start us, length us, event | category | flops | bytes accessed | tf_op | source)
XLA Modules:
  0.0 54.2 jit_solution(6076997412098450641)
XLA Ops:
  0.6 51.6 %shard_map.77 = (f32[4,64,64]{2,1,0:T(8,128)}, f32[4,4,64,64]{3,2,1,0:T(8,128)}) custom-call(bf16[4,6,64,4096]{3,2,1,0:T(8,128)(2,1)} %bitcast.10, bf16[2,6,6,2,4096]{4,3,2,1,0:T(2,128)(2,1)} %bitcast.11, bf16[2,6,6,2,4096]{4,3,2,1,0:T(2,128)(2,1)} %bitcast.12, bf16[2,6,6,2,4096]{4,3,2,1,0:T(2,128)(2,1)} %bitcast.13, s32[4,4,128]{2,1,0:T(4,128)} %bitcast.17, ...), custom_call_target="tpu_custom_call" | custom-call | flops 10000000000 | bytes 17000000 | tf_op jit(solution)/shard_map/pallas_call | solution.py:345
  52.2 2.0 %shard_map.78 = (f32[4,64,64]{2,1,0:T(8,128)}, f32[4,4,64,64]{3,2,1,0:T(8,128)}) custom-call(f32[4,64,64]{2,1,0:T(8,128)} %get-tuple-element.6.diag_in, f32[4,4,64,64]{3,2,1,0:T(8,128)} %get-tuple-element.7.off_in), custom_call_target="tpu_custom_call" | custom-call | tf_op jit(solution)/shard_map/pallas_call | solution.py:370

commit v3 on v2

--- a/solution.py
+++ b/solution.py
@@ -41,8 +41,8 @@
     return col > 0
 
 
-def kernel(dims, z_hbm, jc_hbm, jl_hbm, ju_hbm, cells_ref, couple_ref, diag_ref, off_ref,
-           z, jac, coef, applied, gather, faces, pushed, arrived, load_sem, send_sem, recv_sem):
+def kernel(dims, z_hbm, jc_hbm, jl_hbm, ju_hbm, cells_hbm, couple_hbm, diag_ref, off_ref,
+           z, jac, cells_ref, couple_ref, coef, applied, gather, faces, pushed, arrived, load_sem, small_sem, send_sem, recv_sem):
     nx, ny, comp, kdim, ncell, nface = dims
     subs = nx * ny
     chunks = ncell // WIDE
@@ -61,9 +61,15 @@
         ]
         return [pltpu.make_async_copy(src, dst, load_sem.at[n, m]) for m, (src, dst) in enumerate(pairs)]
 
-    for n in range(4 * nx):
+    small = [
+        pltpu.make_async_copy(src, dst, small_sem.at[n])
+        for n, (src, dst) in enumerate(((cells_hbm, cells_ref), (couple_hbm, couple_ref)))
+    ]
+    small[0].start()
+    for n in range(2):
         for copy in loads(n):
             copy.start()
+    small[1].start()
     barrier = pltpu.get_barrier_semaphore()
     for facing in range(4):
         pl.semaphore_signal(barrier, inc=1, device_id=neighbour_of(facing), device_id_type=MESH)
@@ -119,7 +125,7 @@
                 )
                 ends = pltpu.roll(ends.astype(F32), 2 * b + 1, 1)
                 edges = ends if edges is None else jnp.where(across < 2 * b, edges, ends)
-            edges = edges.astype(BF16)
+            edges = edges.astype(BF16)[:, :16]
             for q in qs:
                 line = []
                 for a in (2 * q, 2 * q + 1):
@@ -127,7 +133,7 @@
                     for b in range(comp):
                         grid = jnp.where((row16 == 2 * b) & (col16 == 0), row(1, a, b, 16), grid)
                         grid = jnp.where((row16 == 2 * b + 1) & (col16 == LANES - 1), row(2, a, b, 16), grid)
-                    line.append(jnp.concatenate([grid, jnp.zeros((LANES - 16, LANES), F32)], axis=0).astype(BF16))
+                    line.append(grid.astype(BF16))
                 add(q, jnp.dot(edges, jnp.concatenate(line, axis=1), preferred_element_type=F32))
 
         def finish(q):
@@ -140,7 +146,7 @@
             steps.append(functools.partial(finish, q))
         return steps
 
-    def stencil(it, side, extra):
+    def stencil(it, side, extra, by_matrix):
         i = it // chunks
         s = i * ny + side
         c0 = pl.multiple_of(lax.rem(it, chunks) * WIDE, WIDE)
@@ -158,7 +164,7 @@
 
         tiles = all_tiles
         slots = {}
-        if side == 0:
+        if by_matrix:
             tiles = all_tiles[: len(all_tiles) // 2]
             matrix = matrix_tile(s, side, 1, pl.multiple_of(c0 + 2 * LANES, LANES))
             for m, step in enumerate(matrix):
@@ -233,18 +239,22 @@
 
         steps = [functools.partial(piece, h) for h in range(2 * quarter // PIECE)]
         weights(it)
-        stencil(it, 0, steps[: len(steps) // 4])
-        stencil(it, 1, steps[len(steps) // 4 :])
+        stencil(it, 0, steps[:1], True)
+        stencil(it, 1, steps[1:], False)
         return carry
 
     def without_faces(it, carry):
         weights(it)
-        stencil(it, 0, [])
-        stencil(it, 1, [])
+        stencil(it, 0, [], True)
+        stencil(it, 1, [], True)
         return carry
 
+    small[0].wait()
     for copy in loads(0):
         copy.wait()
+    for n in range(2, 4 * nx):
+        for copy in loads(n):
+            copy.start()
     lax.fori_loop(0, 8 * nx, with_faces, 0)
 
     def push(s, carry):
@@ -262,6 +272,7 @@
                 pushed[s, d, :, a * nface : (a + 1) * nface] = acc.astype(BF16)
         return carry
 
+    small[1].wait()
     lax.fori_loop(0, subs, push, 0)
 
     pl.semaphore_wait(barrier, 4)
@@ -326,9 +337,18 @@
             off_ref[s, e] = jnp.where(inside, tile(s, e, arrived[d, m]), 0.0)
 
 
-def hand_over(diag_in, off_in, diag_out, off_out):
-    diag_out[...] = diag_in[...]
-    off_out[...] = off_in[...]
+def hand_over(diag_in, off_in, diag_out, off_out, diag, off, sems):
+    parts = [(diag_in, diag, diag_out)]
+    parts += [(off_in.at[s], off.at[s], off_out.at[s]) for s in range(off_in.shape[0])]
+    reads = [pltpu.make_async_copy(a, b, sems.at[0, n]) for n, (a, b, _) in enumerate(parts)]
+    writes = [pltpu.make_async_copy(b, c, sems.at[1, n]) for n, (_, b, c) in enumerate(parts)]
+    for copy in reads:
+        copy.start()
+    for read, write in zip(reads, writes):
+        read.wait()
+        write.start()
+    for copy in writes:
+        copy.wait()
 
 
 def on_device(z_basis, jac_center, jac_lower, jac_upper, face_cells, couple):
@@ -345,11 +365,13 @@
     results = pl.pallas_call(
         functools.partial(kernel, (nx, ny, comp, kdim, ncell, nface)),
         out_shape=shapes,
-        in_specs=[pl.BlockSpec(memory_space=pl.ANY)] * 4 + [pl.BlockSpec(memory_space=pltpu.VMEM)] * 2,
+        in_specs=[pl.BlockSpec(memory_space=pl.ANY)] * 6,
         out_specs=[pl.BlockSpec(memory_space=pltpu.VMEM)] * 2,
         scratch_shapes=[
             pltpu.VMEM((subs, comp, kdim, ncell + 2 * LANES), BF16),
             pltpu.VMEM((3, nx, comp, comp, ny, ncell), BF16),
+            pltpu.VMEM((subs, 4, nface), jnp.int32),
+            pltpu.VMEM((subs, comp, comp, 4, nface), BF16),
             pltpu.VMEM((3, comp, comp, ny, WIDE), F32),
             pltpu.VMEM((2, comp, kdim, WIDE), BF16),
             pltpu.VMEM((subs, 2, comp * kdim, 2 * nface), F32),
@@ -357,6 +379,7 @@
             pltpu.VMEM((subs, 4, kdim, wide), BF16),
             pltpu.VMEM((4, 2, kdim, wide), BF16),
             pltpu.SemaphoreType.DMA((4 * nx, 3 + ny)),
+            pltpu.SemaphoreType.DMA((2,)),
             pltpu.SemaphoreType.DMA((4, 2)),
             pltpu.SemaphoreType.DMA((4, 2)),
         ],
@@ -370,8 +393,14 @@
     diag, off = pl.pallas_call(
         hand_over,
         out_shape=shapes,
-        in_specs=[pl.BlockSpec(memory_space=pltpu.VMEM)] * 2,
-        out_specs=[pl.BlockSpec(memory_space=pltpu.VMEM)] * 2,
+        in_specs=[pl.BlockSpec(memory_space=pl.ANY)] * 2,
+        out_specs=[pl.BlockSpec(memory_space=pl.ANY)] * 2,
+        scratch_shapes=[
+            pltpu.VMEM(shapes[0].shape, F32),
+            pltpu.VMEM(shapes[1].shape, F32),
+            pltpu.SemaphoreType.DMA((2, 1 + subs)),
+        ],
+        compiler_params=pltpu.CompilerParams(vmem_limit_bytes=56 * 2**20),
     )(*results)
     return diag.reshape(nx, ny, kdim, kdim), off.reshape(nx, ny, 4, kdim, kdim)
 

time: 54.3 us -> 52.9 us (0.974)
  Pallas kernels: 53.5 us -> 52.1 us
    pallas_call x1, Pallas kernels: 51.6 us -> 50.2 us  [on_device(): pl.pallas_call(functools.partial(kernel, (nx, ny, comp, kdim, ncell, nfac...]
where the time goes in v3:
time: 52.9 us; the launch traced here: 52.8 us
  Pallas kernels  52.1 us (98%)
  between operations  0.64 us (1%)
    pallas_call x1, Pallas kernels, on_device(): pl.pallas_call(functools.partial(kernel, (nx, ny, comp, kdim, ncell, nfac...  50.2 us
    pallas_call x1, Pallas kernels, on_device(): pl.pallas_call(hand_over, out_shape=shapes, in_specs=[pl.BlockSpec(memory...  1.91 us

profile of v3, /device:TPU:3, one launch (start us, length us, event | category | flops | bytes accessed | tf_op | source)
XLA Modules:
  0.0 52.8 jit_solution(9025719782196452005)
XLA Ops:
  0.6 50.2 %shard_map.77 = (f32[4,64,64]{2,1,0:T(8,128)}, f32[4,4,64,64]{3,2,1,0:T(8,128)}) custom-call(bf16[4,6,64,4096]{3,2,1,0:T(8,128)(2,1)} %bitcast.10, bf16[2,6,6,2,4096]{4,3,2,1,0:T(2,128)(2,1)} %bitcast.11, bf16[2,6,6,2,4096]{4,3,2,1,0:T(2,128)(2,1)} %bitcast.12, bf16[2,6,6,2,4096]{4,3,2,1,0:T(2,128)(2,1)} %bitcast.13, s32[4,4,128]{2,1,0:T(4,128)} %bitcast.17, ...), custom_call_target="tpu_custom_call" | custom-call | flops 10000000000 | bytes 17000000 | tf_op jit(solution)/shard_map/pallas_call | solution.py:365
  50.9 1.9 %shard_map.78 = (f32[4,64,64]{2,1,0:T(8,128)}, f32[4,4,64,64]{3,2,1,0:T(8,128)}) custom-call(f32[4,64,64]{2,1,0:T(8,128)} %get-tuple-element.6.diag_in, f32[4,4,64,64]{3,2,1,0:T(8,128)} %get-tuple-element.7.off_in), custom_call_target="tpu_custom_call" | custom-call | tf_op jit(solution)/shard_map/pallas_call | solution.py:393

commit v4 on v3

--- a/solution.py
+++ b/solution.py
@@ -172,7 +172,7 @@
         for a in range(comp):
             slots.setdefault(a * len(tiles) // comp, []).append(functools.partial(tile_dot, a))
         for m, step in enumerate(extra):
-            slots.setdefault((2 * m + 1) * len(tiles) // (2 * len(extra)), []).append(step)
+            slots.setdefault(m * len(tiles) // len(extra), []).append(step)
 
         for m, (t, k0) in enumerate(tiles):
             for step in slots.get(m, []):
@@ -273,7 +273,18 @@
         return carry
 
     small[1].wait()
-    lax.fori_loop(0, subs, push, 0)
+    def tile(s, e, right):
+        return lax.dot_general(faces[s, e], right, NT, preferred_element_type=F32)
+
+    steps_of = ((1, 0), (-1, 0), (0, 1), (0, -1))
+    for s in range(subs):
+        push(s, 0)
+        for e in range(4):
+            ti, tj = s // ny + steps_of[e][0], s % ny + steps_of[e][1]
+            other = ti * ny + tj
+            if 0 <= ti < nx and 0 <= tj < ny and other < s:
+                off_ref[s, e] = tile(s, e, pushed[other, OPPOSITE[e]])
+                off_ref[other, OPPOSITE[e]] = tile(other, OPPOSITE[e], pushed[s, e])
 
     pl.semaphore_wait(barrier, 4)
 
@@ -318,16 +329,6 @@
     for s in range(subs):
         diag_ref[s] = diag_ref[s].T
 
-    def tile(s, e, right):
-        return lax.dot_general(faces[s, e], right, NT, preferred_element_type=F32)
-
-    steps_of = ((1, 0), (-1, 0), (0, 1), (0, -1))
-    for i in range(nx):
-        for j in range(ny):
-            for e in range(4):
-                ti, tj = i + steps_of[e][0], j + steps_of[e][1]
-                if 0 <= ti < nx and 0 <= tj < ny:
-                    off_ref[i * ny + j, e] = tile(i * ny + j, e, pushed[ti * ny + tj, OPPOSITE[e]])
     for copy in sends:
         copy.wait()
     for e in range(4):

time: 52.9 us -> 52.8 us (level)
  no operation moved by 1% of the time
where the time goes in v4:
time: 52.8 us; the launch traced here: 52.7 us
  Pallas kernels  52 us (98%)
  between operations  0.64 us (1%)
    pallas_call x1, Pallas kernels, on_device(): pl.pallas_call(functools.partial(kernel, (nx, ny, comp, kdim, ncell, nfac...  50.1 us
    pallas_call x1, Pallas kernels, on_device(): pl.pallas_call(hand_over, out_shape=shapes, in_specs=[pl.BlockSpec(memory...  1.91 us

profile of v4, /device:TPU:3, one launch (start us, length us, event | category | flops | bytes accessed | tf_op | source)
XLA Modules:
  0.0 52.7 jit_solution(6146723121990049452)
XLA Ops:
  0.6 50.1 %shard_map.77 = (f32[4,64,64]{2,1,0:T(8,128)}, f32[4,4,64,64]{3,2,1,0:T(8,128)}) custom-call(bf16[4,6,64,4096]{3,2,1,0:T(8,128)(2,1)} %bitcast.10, bf16[2,6,6,2,4096]{4,3,2,1,0:T(2,128)(2,1)} %bitcast.11, bf16[2,6,6,2,4096]{4,3,2,1,0:T(2,128)(2,1)} %bitcast.12, bf16[2,6,6,2,4096]{4,3,2,1,0:T(2,128)(2,1)} %bitcast.13, s32[4,4,128]{2,1,0:T(4,128)} %bitcast.17, ...), custom_call_target="tpu_custom_call" | custom-call | flops 10000000000 | bytes 17000000 | tf_op jit(solution)/shard_map/pallas_call | solution.py:366
  50.8 1.9 %shard_map.78 = (f32[4,64,64]{2,1,0:T(8,128)}, f32[4,4,64,64]{3,2,1,0:T(8,128)}) custom-call(f32[4,64,64]{2,1,0:T(8,128)} %get-tuple-element.6.diag_in, f32[4,4,64,64]{3,2,1,0:T(8,128)} %get-tuple-element.7.off_in), custom_call_target="tpu_custom_call" | custom-call | tf_op jit(solution)/shard_map/pallas_call | solution.py:394

commit v5 on v4

--- a/solution.py
+++ b/solution.py
@@ -255,7 +255,6 @@
     for n in range(2, 4 * nx):
         for copy in loads(n):
             copy.start()
-    lax.fori_loop(0, 8 * nx, with_faces, 0)
 
     def push(s, carry):
         for d in range(4):
@@ -272,21 +271,10 @@
                 pushed[s, d, :, a * nface : (a + 1) * nface] = acc.astype(BF16)
         return carry
 
-    small[1].wait()
     def tile(s, e, right):
         return lax.dot_general(faces[s, e], right, NT, preferred_element_type=F32)
 
     steps_of = ((1, 0), (-1, 0), (0, 1), (0, -1))
-    for s in range(subs):
-        push(s, 0)
-        for e in range(4):
-            ti, tj = s // ny + steps_of[e][0], s % ny + steps_of[e][1]
-            other = ti * ny + tj
-            if 0 <= ti < nx and 0 <= tj < ny and other < s:
-                off_ref[s, e] = tile(s, e, pushed[other, OPPOSITE[e]])
-                off_ref[other, OPPOSITE[e]] = tile(other, OPPOSITE[e], pushed[s, e])
-
-    pl.semaphore_wait(barrier, 4)
 
     def sources(d):
         if d == 0:
@@ -297,9 +285,10 @@
             return [i * ny + ny - 1 for i in range(nx)]
         return [i * ny for i in range(nx)]
 
-    sends = []
+    sends, start_of = [], []
     for d in range(4):
         for m, s in enumerate(sources(d)):
+            start_of.append(s)
             sends.append(
                 pltpu.make_async_remote_copy(
                     src_ref=pushed.at[s, d],
@@ -310,8 +299,22 @@
                     device_id_type=MESH,
                 )
             )
-    for copy in sends:
-        copy.start()
+    for i in range(nx):
+        lax.fori_loop(8 * i, 8 * (i + 1), with_faces, 0)
+        if i == 0:
+            small[1].wait()
+            pl.semaphore_wait(barrier, 4)
+        for s in range(i * ny, (i + 1) * ny):
+            push(s, 0)
+            for e in range(4):
+                ti, tj = s // ny + steps_of[e][0], s % ny + steps_of[e][1]
+                other = ti * ny + tj
+                if 0 <= ti < nx and 0 <= tj < ny and other < s:
+                    off_ref[s, e] = tile(s, e, pushed[other, OPPOSITE[e]])
+                    off_ref[other, OPPOSITE[e]] = tile(other, OPPOSITE[e], pushed[s, e])
+            for start, copy in zip(start_of, sends):
+                if start == s:
+                    copy.start()
 
     lax.fori_loop(8 * nx, nx * chunks, without_faces, 0)
 

time: 52.8 us -> 52.9 us (level)
  no operation moved by 1% of the time
where the time goes in v5:
time: 52.9 us; the launch traced here: 52.8 us
  Pallas kernels  52.1 us (98%)
  between operations  0.64 us (1%)
    pallas_call x1, Pallas kernels, on_device(): pl.pallas_call(functools.partial(kernel, (nx, ny, comp, kdim, ncell, nfac...  50.2 us
    pallas_call x1, Pallas kernels, on_device(): pl.pallas_call(hand_over, out_shape=shapes, in_specs=[pl.BlockSpec(memory...  1.91 us

profile of v5, /device:TPU:3, one launch (start us, length us, event | category | flops | bytes accessed | tf_op | source)
XLA Modules:
  0.0 52.8 jit_solution(12179682351259700807)
XLA Ops:
  0.6 50.2 %shard_map.77 = (f32[4,64,64]{2,1,0:T(8,128)}, f32[4,4,64,64]{3,2,1,0:T(8,128)}) custom-call(bf16[4,6,64,4096]{3,2,1,0:T(8,128)(2,1)} %bitcast.10, bf16[2,6,6,2,4096]{4,3,2,1,0:T(2,128)(2,1)} %bitcast.11, bf16[2,6,6,2,4096]{4,3,2,1,0:T(2,128)(2,1)} %bitcast.12, bf16[2,6,6,2,4096]{4,3,2,1,0:T(2,128)(2,1)} %bitcast.13, s32[4,4,128]{2,1,0:T(4,128)} %bitcast.17, ...), custom_call_target="tpu_custom_call" | custom-call | flops 10000000000 | bytes 17000000 | tf_op jit(solution)/shard_map/pallas_call | solution.py:369
  50.9 1.9 %shard_map.78 = (f32[4,64,64]{2,1,0:T(8,128)}, f32[4,4,64,64]{3,2,1,0:T(8,128)}) custom-call(f32[4,64,64]{2,1,0:T(8,128)} %get-tuple-element.6.diag_in, f32[4,4,64,64]{3,2,1,0:T(8,128)} %get-tuple-element.7.off_in), custom_call_target="tpu_custom_call" | custom-call | tf_op jit(solution)/shard_map/pallas_call | solution.py:397
